TPU v7x, 128 devices: a whole 4x4x4 slice. The times are simulated.
128 devices in a mesh: row: 8 (over y, core), col: 16 (over z, x).
Axes of the slice: x: 4, y: 4, z: 4, core: 2. Of those that a mesh axis runs over, the one named last changes fastest.
Arguments:
- sigma_top: float32 [6144, 6144], P('row', 'col')
- factor_cross: float32 [6144, 6144], P('row', 'col'), may hold values from -0.078125 to 0.078125
- factor_inverse: float32 [6144, 6144], P('row', 'col')
- block_inverse: float32 [6144, 6144], P('row', 'col')
- ancestors: int32 [12], replicated, may hold values from 0 to 23, as said below
Outputs:
- sigma_cross: float32 [6144, 6144], P('row', 'col')
- sigma_child: float32 [6144, 6144], P('row', 'col')
Inputs may be any that keep to these rules, and one draw needn't show every extreme that they name: `ancestors`: 12 distinct block numbers; block 0 and block 23 are always among them.
All inputs are finite; a program needn't handle non-finite values.
Results may differ from a plain program's by a relative error of at most 0.000078.
Values sent between devices are 32-bit elements; how exact they have to be, the bound alone decides.
No kernel may reach another device: no remote copies, remote signals or barrier semaphores. Data moves between devices by JAX's collectives and lax.ppermute only.
A program may use at most 128 MiB of HBM per device.

v0:
```python
import jax
import jax.numpy as jnp
import numpy as np
from jax import lax
from jax.sharding import Mesh, PartitionSpec as P

NB = 24
NANC = 12
ROW = ("y", "core")
COL = ("z", "x")
ALL = ("y", "core", "z", "x")


def shift(x, axis, n, k):
    return lax.ppermute(x, axis, [(i, (i + k) % n) for i in range(n)])


def gather_rows(x):
    y, core = (lax.axis_index("y"), lax.axis_index("core"))
    half = x.shape[0] // 2
    left = shift(x, "y", 4, 1)
    right = shift(x, "y", 4, -1)
    far = jnp.concatenate([shift(left[:half], "y", 4, 1), shift(right[half:], "y", 4, -1)])
    mine = [x, left, right, far]
    at = [y, (y + 3) % 4, (y + 1) % 4, (y + 2) % 4]
    out = [(2 * a + core, t) for a, t in zip(at, mine)]
    out += [(2 * a + 1 - core, shift(t, "core", 2, 1)) for a, t in zip(at, mine)]
    return out


def spread(x):
    h, w = x.shape
    sub = h // 24
    return lax.all_to_all(x.reshape(3, 8, sub, w), ROW, 1, 0, tiled=True).reshape(NB, sub, w)


def pick(x, ancestors):
    return jnp.concatenate([lax.dynamic_slice_in_dim(x, ancestors[i], 1, 0) for i in range(NANC)])


def dot(a, b, dims):
    return lax.dot_general(
        a, b, (dims, ((), ())), precision=lax.Precision.HIGH, preferred_element_type=jnp.float32
    )


def per_device(sigma_top, factor_cross, factor_inverse, block_inverse, ancestors):
    h, w = sigma_top.shape
    sub = h // 24
    part = NANC * sub
    f = pick(spread(factor_cross), ancestors).reshape(part, w)
    f_all = lax.all_gather(f, COL, axis=1, tiled=True)
    strip = jnp.zeros((8 * h, w), jnp.float32)
    for r, t in gather_rows(factor_inverse):
        strip = lax.dynamic_update_slice(strip, t, (r * h, 0))
    s = pick(spread(sigma_top), ancestors).reshape(part, w)
    s_all = lax.all_gather(s, COL, axis=1, tiled=True)
    u = dot(f_all, strip, ((1,), (0,)))
    moved = lax.ppermute(
        u, ALL, [(16 * r + c, 16 * (c // 2) + 2 * r + c % 2) for r in range(8) for c in range(16)]
    )
    u_side = lax.all_gather(moved, COL, axis=0, tiled=False).reshape(8, 2, part, w)
    u_col = jnp.zeros((NANC, 8, sub, w), jnp.float32)
    for r, t in gather_rows(u):
        u_col = lax.dynamic_update_slice(u_col, t.reshape(NANC, 1, sub, w), (0, r, 0, 0))
    s_sel = jnp.concatenate(
        [lax.dynamic_slice_in_dim(s_all, ancestors[i] * 8 * sub, 8 * sub, 1) for i in range(NANC)],
        axis=1,
    )
    sigma = -dot(s_sel, u_col.reshape(8 * part, w), ((1,), (0,)))
    sigma_col = jnp.zeros((8, part, w), jnp.float32)
    for r, t in gather_rows(sigma):
        sigma_col = lax.dynamic_update_slice(sigma_col, t[None], (r, 0, 0))
    correction = jnp.concatenate([dot(u_side[:, p], sigma_col, ((0, 1), (0, 1))) for p in range(2)])
    sigma_child = block_inverse - correction
    blocks = sigma.reshape(NANC, sub, w)
    hit = ancestors[None, :] == lax.iota(jnp.int32, NB)[:, None]
    place = jnp.argmax(hit, axis=1)
    living = jnp.any(hit, axis=1)
    full = jnp.concatenate([lax.dynamic_slice_in_dim(blocks, place[b], 1, 0) for b in range(NB)])
    full = jnp.where(living[:, None, None], full, jnp.float32(0.0))
    back = lax.all_to_all(full.reshape(8, 3, sub, w), ROW, 0, 0, tiled=True)
    sigma_cross = back.reshape(8, 3, sub, w).transpose(1, 0, 2, 3).reshape(h, w)
    return (sigma_cross, sigma_child)


def solution(mesh):
    fine = Mesh(np.asarray(mesh.devices).reshape(4, 2, 4, 4), ALL)
    tile = P(ROW, COL)
    return jax.shard_map(
        per_device,
        mesh=fine,
        in_specs=(tile, tile, tile, tile, P()),
        out_specs=(tile, tile),
        check_vma=False,
    )
```

profile of v0, /device:TPU:1, one launch (start us, length us, event | category | flops | bytes accessed | tf_op | source)
XLA Modules:
  0.0 343.1 jit_solution(14482909959101323158)
XLA Ops:
  7.2 2.5 copy.63
  9.6 6.0 %all-to-all-start.1 = ((f32[3,8,32,384]{3,2,0,1:T(8,128)}), f32[3,8,32,384]{3,2,0,1:T(8,128)S(1)}, u32[]{:S(2)}, u32[]{:S(2)}) async-start(f32[3,8,32,384]{3,2,0,1:T(8,128)} %copy.63), calls=%async_computation.1 | async-start | bytes 2359296 | tf_op jit(solution)/shard_map/all_to_all | solution.py:34
  16.7 15.4 %all-to-all-done.1 = f32[3,8,32,384]{3,2,0,1:T(8,128)S(1)} async-done(((f32[3,8,32,384]{3,2,0,1:T(8,128)}), f32[3,8,32,384]{3,2,0,1:T(8,128)S(1)}, u32[]{:S(2)}, u32[]{:S(2)}) %all-to-all-start.1) | async-done | bytes 1179680 | tf_op jit(solution)/shard_map/all_to_all | solution.py:34
  32.1 4.3 %all-to-all-start = ((f32[3,8,32,384]{3,2,0,1:T(8,128)}), f32[3,8,32,384]{3,2,0,1:T(8,128)S(1)}, u32[]{:S(2)}, u32[]{:S(2)}) async-start(f32[3,8,32,384]{3,2,0,1:T(8,128)} %copy.62), calls=%async_computation | async-start | bytes 2359296 | tf_op jit(solution)/shard_map/all_to_all | solution.py:34
  64.1 26.1 %collective-permute-done = f32[768,384]{1,0:T(8,128)S(1)} collective-permute-done((f32[768,384]{1,0:T(8,128)}, f32[768,384]{1,0:T(8,128)S(1)}, u32[]{:S(2)}, u32[]{:S(2)}) %collective-permute-start) | collective-permute-done | bytes 1179680 | tf_op jit(solution)/shard_map/ppermute | solution.py:15
  90.4 2.7 collective-permute-start.3
  95.2 10.4 %collective-permute-done.2 = f32[384,384]{1,0:T(8,128)S(1)} collective-permute-done((f32[384,384]{1,0:T(8,128)S(1)}, f32[384,384]{1,0:T(8,128)S(1)}, u32[]{:S(2)}, u32[]{:S(2)}) %collective-permute-start.2) | collective-permute-done | bytes 589856 | tf_op jit(solution)/shard_map/ppermute | solution.py:15
  107.5 4.3 %broadcast_in_dim.53 = f32[6144,384]{1,0:T(8,128)} broadcast(f32[]{:T(128)} %constant.74.clone.1), dimensions={} | broadcast | bytes 9437188 | tf_op jit(solution)/shard_map/broadcast_in_dim | solution.py:53
  111.8 2.4 constant_dynamic-update-slice_fusion.69
  117.5 2.4 constant_dynamic-update-slice_fusion.65
  120.0 2.4 constant_dynamic-update-slice_fusion.64
  122.4 2.4 constant_dynamic-update-slice_fusion.63
  124.8 2.4 constant_dynamic-update-slice_fusion.62
  127.2 11.1 %all-gather.7.cloned.1.call-done = f32[384,6144]{1,0:T(8,128)} async-done(((f32[384,384]{1,0:T(8,128)}), f32[384,6144]{1,0:T(8,128)}) %all-gather.7.cloned.1.call-update) | async-done | bytes 9437200 | tf_op jit(solution)/shard_map/all_gather | solution.py:52
  138.3 11.7 %fusion.8 = f32[384,384]{1,0:T(8,128)S(1)} fusion(f32[384,6144]{1,0:T(8,128)} %all-gather.7.cloned.1.call-done, f32[6144,384]{1,0:T(8,128)} %constant_dynamic-update-slice_fusion.62), kind=kOutput, calls=%fused_computation.105 | convolution fusion | flops 5435817984 | bytes 19464192 | tf_op jit(solution)/shard_map/dot_general | solution.py:42
  150.0 5.2 %collective-permute-start.16 = (f32[384,384]{1,0:T(8,128)S(1)}, f32[384,384]{1,0:T(8,128)S(1)}, u32[]{:S(2)}, u32[]{:S(2)}) collective-permute-start(f32[384,384]{1,0:T(8,128)S(1)} %fusion.8), channel_id=1, source_target_pairs={{0,0},{1,1},{2,16},{3,17},{4,32},{5,33},{6,48},{7,49},{8,64},{9,65... | collective-permute-start | bytes 1769480 | tf_op jit(solution)/shard_map/ppermute | solution.py:59
  155.2 14.5 %collective-permute-done.16 = f32[384,384]{1,0:T(8,128)S(1)} collective-permute-done((f32[384,384]{1,0:T(8,128)S(1)}, f32[384,384]{1,0:T(8,128)S(1)}, u32[]{:S(2)}, u32[]{:S(2)}) %collective-permute-start.16) | collective-permute-done | bytes 589856 | tf_op jit(solution)/shard_map/ppermute | solution.py:59
  225.2 4.2 %collective-permute-start.8 = (f32[384,384]{1,0:T(8,128)S(1)}, f32[384,384]{1,0:T(8,128)S(1)}, u32[]{:S(2)}, u32[]{:S(2)}) collective-permute-start(f32[384,384]{1,0:T(8,128)S(1)} %fusion.8), channel_id=1, source_target_pairs={{0,32},{32,64},{64,96},{96,0},{1,33},{33,65},{65,97},{97,1},{2,34}... | collective-permute-start | bytes 1769480 | tf_op jit(solution)/shard_map/ppermute | solution.py:15
  229.4 4.4 %collective-permute-start.9 = (f32[384,384]{1,0:T(8,128)S(1)}, f32[384,384]{1,0:T(8,128)S(1)}, u32[]{:S(2)}, u32[]{:S(2)}) collective-permute-start(f32[384,384]{1,0:T(8,128)S(1)} %fusion.8), channel_id=1, source_target_pairs={{0,96},{32,0},{64,32},{96,64},{1,97},{33,1},{65,33},{97,65},{2,98}... | collective-permute-start | bytes 1769480 | tf_op jit(solution)/shard_map/ppermute | solution.py:15
  233.8 9.4 %collective-permute-start.12 = (f32[384,384]{1,0:T(8,128)S(1)}, f32[384,384]{1,0:T(8,128)S(1)}, u32[]{:S(2)}, u32[]{:S(2)}) collective-permute-start(f32[384,384]{1,0:T(8,128)S(1)} %fusion.8), channel_id=1, source_target_pairs={{0,16},{16,0},{1,17},{17,1},{2,18},{18,2},{3,19},{19,3},{4,20},{20... | collective-permute-start | bytes 1769480 | tf_op jit(solution)/shard_map/ppermute | solution.py:15
  255.5 2.7 collective-permute-start.11
  260.1 4.4 %collective-permute-done.10 = f32[192,384]{1,0:T(8,128)S(1)} collective-permute-done((f32[192,384]{1,0:T(8,128)S(1)}, f32[192,384]{1,0:T(8,128)S(1)}, u32[]{:S(2)}, u32[]{:S(2)}) %collective-permute-start.10) | collective-permute-done | bytes 294944 | tf_op jit(solution)/shard_map/ppermute | solution.py:15
  267.3 2.5 broadcast_in_dim.55
  269.8 5.0 %bitcast_dynamic-update-slice_fusion.7 = (f32[8,384,384]{2,1,0:T(8,128)}, f32[384,384]{1,0:T(8,128)S(1)}) fusion(f32[8,384,384]{2,1,0:T(8,128)} %broadcast_in_dim.55, s32[]{:T(128)S(6)} %select_n.283, f32[384,3072]{1,0:T(8,128)S(1)} %dynamic-slice_dynamic-update-slice_fusion, f32[3072,384]{1,0:T(8,128)S(1)} %bitcast.119), kind=kOutput, calls=%fused_computation.15 | convolution fusion | flops 2718056448 | bytes 10616836 | tf_op jit(solution)/shard_map/dot_general | solution.py:42
  275.4 2.9 collective-permute-start.18
  280.5 3.5 %all-to-all-start.2 = ((f32[8,3,32,384]{3,2,1,0:T(8,128)}), f32[8,3,32,384]{3,2,1,0:T(8,128)S(1)}, u32[]{:S(2)}, u32[]{:S(2)}) async-start(f32[8,3,32,384]{3,2,1,0:T(8,128)} %broadcast_select_fusion), calls=%async_computation.2 | async-start | bytes 2359296 | tf_op jit(solution)/shard_map/all_to_all | solution.py:82
  284.0 7.7 %collective-permute-done.17 = f32[384,384]{1,0:T(8,128)S(1)} collective-permute-done((f32[384,384]{1,0:T(8,128)S(1)}, f32[384,384]{1,0:T(8,128)S(1)}, u32[]{:S(2)}, u32[]{:S(2)}) %collective-permute-start.17) | collective-permute-done | bytes 589856 | tf_op jit(solution)/shard_map/ppermute | solution.py:15
  292.0 3.7 %collective-permute-start.20 = (f32[192,384]{1,0:T(8,128)S(1)}, f32[192,384]{1,0:T(8,128)S(1)}, u32[]{:S(2)}, u32[]{:S(2)}) collective-permute-start(f32[192,384]{1,0:T(8,128)S(1)} %slice.206), channel_id=1, source_target_pairs={{0,96},{32,0},{64,32},{96,64},{1,97},{33,1},{65,33},{97,65},{2,98}... | collective-permute-start | bytes 884744 | tf_op jit(solution)/shard_map/ppermute | solution.py:15
  295.8 2.2 collective-permute-start.22
  299.6 11.1 %collective-permute-done.19 = f32[192,384]{1,0:T(8,128)S(1)} collective-permute-done((f32[192,384]{1,0:T(8,128)S(1)}, f32[192,384]{1,0:T(8,128)S(1)}, u32[]{:S(2)}, u32[]{:S(2)}) %collective-permute-start.19) | collective-permute-done | bytes 294944 | tf_op jit(solution)/shard_map/ppermute | solution.py:15
  321.5 7.8 %fusion.2 = f32[384,384]{1,0:T(8,128)S(1)} fusion(f32[8,384,384]{2,1,0:T(8,128)} %bitcast_dynamic-update-slice_fusion, f32[8,2,384,384]{3,2,1,0:T(8,128)} %bitcast.120), kind=kOutput, calls=%fused_computation.4 | convolution fusion | flops 2717908992 | bytes 10027008 | tf_op jit(solution)/shard_map/dot_general | solution.py:42
  329.3 6.1 %fusion.3 = f32[384,384]{1,0:T(8,128)S(1)} fusion(f32[8,384,384]{2,1,0:T(8,128)} %bitcast_dynamic-update-slice_fusion, f32[8,2,384,384]{3,2,1,0:T(8,128)S(1)} %bitcast.121), kind=kOutput, calls=%fused_computation.5 | convolution fusion | flops 2717908992 | bytes 10027008 | tf_op jit(solution)/shard_map/dot_general | solution.py:42
  (159 shorter events, 50.5 us)
Async XLA Ops:
  7.2 29.3 %copy-start.6 = (s32[12]{0:T(128)S(1)}, s32[12]{0:T(128)}, u32[]{:S(2)}) copy-start(s32[12]{0:T(128)} %param.9) | copy-start | bytes 148
  9.6 22.5 %all-to-all-start.1 = ((f32[3,8,32,384]{3,2,0,1:T(8,128)}), f32[3,8,32,384]{3,2,0,1:T(8,128)S(1)}, u32[]{:S(2)}, u32[]{:S(2)}) async-start(f32[3,8,32,384]{3,2,0,1:T(8,128)} %copy.63), calls=%async_computation.1 | async-start | bytes 2359296 | tf_op jit(solution)/shard_map/all_to_all | solution.py:34
  32.1 26.9 %all-to-all-start = ((f32[3,8,32,384]{3,2,0,1:T(8,128)}), f32[3,8,32,384]{3,2,0,1:T(8,128)S(1)}, u32[]{:S(2)}, u32[]{:S(2)}) async-start(f32[3,8,32,384]{3,2,0,1:T(8,128)} %copy.62), calls=%async_computation | async-start | bytes 2359296 | tf_op jit(solution)/shard_map/all_to_all | solution.py:34
  36.5 101.8 %all-gather.7.cloned.1.call-start = ((), (), s32[]{:S(2)}) async-start(), calls=%async_computation.4 | async-start | bytes 10027008 | tf_op jit(solution)/shard_map/all_gather | solution.py:52
  60.2 183.0 %all-gather.5.cloned.1.call-start = ((), (), s32[]{:S(2)}) async-start(), calls=%async_computation.3 | async-start | bytes 10027008 | tf_op jit(solution)/shard_map/all_gather | solution.py:57
  61.3 260.2 %all-gather.9.cloned.1.call-start = ((), (), s32[]{:S(2)}) async-start(), calls=%async_computation.5 | async-start | bytes 10027008 | tf_op jit(solution)/shard_map/all_gather | solution.py:62
  61.3 28.9 %collective-permute-start = (f32[768,384]{1,0:T(8,128)}, f32[768,384]{1,0:T(8,128)S(1)}, u32[]{:S(2)}, u32[]{:S(2)}) collective-permute-start(f32[768,384]{1,0:T(8,128)} %param.7), channel_id=1, source_target_pairs={{0,32},{32,64},{64,96},{96,0},{1,33},{33,65},{65,97},{97,1},{2,34}... | collective-permute-start | bytes 3538952 | tf_op jit(solution)/shard_map/ppermute | solution.py:15
  62.8 27.6 %collective-permute-start.1 = (f32[768,384]{1,0:T(8,128)}, f32[768,384]{1,0:T(8,128)S(1)}, u32[]{:S(2)}, u32[]{:S(2)}) collective-permute-start(f32[768,384]{1,0:T(8,128)} %param.7), channel_id=1, source_target_pairs={{0,96},{32,0},{64,32},{96,64},{1,97},{33,1},{65,33},{97,65},{2,98}... | collective-permute-start | bytes 3538952 | tf_op jit(solution)/shard_map/ppermute | solution.py:15
  90.3 15.3 %collective-permute-start.2 = (f32[384,384]{1,0:T(8,128)S(1)}, f32[384,384]{1,0:T(8,128)S(1)}, u32[]{:S(2)}, u32[]{:S(2)}) collective-permute-start(f32[384,384]{1,0:T(8,128)S(1)} %slice.200), channel_id=1, source_target_pairs={{0,32},{32,64},{64,96},{96,0},{1,33},{33,65},{65,97},{97,1},{2,34}... | collective-permute-start | bytes 1769480 | tf_op jit(solution)/shard_map/ppermute | solution.py:15
  90.4 15.2 %collective-permute-start.3 = (f32[384,384]{1,0:T(8,128)S(1)}, f32[384,384]{1,0:T(8,128)S(1)}, u32[]{:S(2)}, u32[]{:S(2)}) collective-permute-start(f32[384,384]{1,0:T(8,128)S(1)} %slice.201), channel_id=1, source_target_pairs={{0,96},{32,0},{64,32},{96,64},{1,97},{33,1},{65,33},{97,65},{2,98}... | collective-permute-start | bytes 1769480 | tf_op jit(solution)/shard_map/ppermute | solution.py:15
  93.1 24.4 %collective-permute-start.4 = (f32[768,384]{1,0:T(8,128)}, f32[768,384]{1,0:T(8,128)}, u32[]{:S(2)}, u32[]{:S(2)}) collective-permute-start(f32[768,384]{1,0:T(8,128)} %param.7), channel_id=1, source_target_pairs={{0,16},{16,0},{1,17},{17,1},{2,18},{18,2},{3,19},{19,3},{4,20},{20... | collective-permute-start | bytes 3538952 | tf_op jit(solution)/shard_map/ppermute | solution.py:15
  94.7 25.3 %collective-permute-start.5 = (f32[768,384]{1,0:T(8,128)S(1)}, f32[768,384]{1,0:T(8,128)}, u32[]{:S(2)}, u32[]{:S(2)}) collective-permute-start(f32[768,384]{1,0:T(8,128)S(1)} %collective-permute-done), channel_id=1, source_target_pairs={{0,16},{16,0},{1,17},{17,1},{2,18},{18,2},{3,19},{19,3},{4,20},{20... | collective-permute-start | bytes 3538952 | tf_op jit(solution)/shard_map/ppermute | solution.py:15
  94.7 27.7 %collective-permute-start.6 = (f32[768,384]{1,0:T(8,128)S(1)}, f32[768,384]{1,0:T(8,128)}, u32[]{:S(2)}, u32[]{:S(2)}) collective-permute-start(f32[768,384]{1,0:T(8,128)S(1)} %collective-permute-done.1), channel_id=1, source_target_pairs={{0,16},{16,0},{1,17},{17,1},{2,18},{18,2},{3,19},{19,3},{4,20},{20... | collective-permute-start | bytes 3538952 | tf_op jit(solution)/shard_map/ppermute | solution.py:15
  105.6 19.2 %collective-permute-start.7 = (f32[768,384]{1,0:T(8,128)S(1)}, f32[768,384]{1,0:T(8,128)}, u32[]{:S(2)}, u32[]{:S(2)}) collective-permute-start(f32[768,384]{1,0:T(8,128)S(1)} %constant_dynamic-update-slice_fusion.24), channel_id=1, source_target_pairs={{0,16},{16,0},{1,17},{17,1},{2,18},{18,2},{3,19},{19,3},{4,20},{20... | collective-permute-start | bytes 3538952 | tf_op jit(solution)/shard_map/ppermute | solution.py:15
  150.0 19.7 %collective-permute-start.16 = (f32[384,384]{1,0:T(8,128)S(1)}, f32[384,384]{1,0:T(8,128)S(1)}, u32[]{:S(2)}, u32[]{:S(2)}) collective-permute-start(f32[384,384]{1,0:T(8,128)S(1)} %fusion.8), channel_id=1, source_target_pairs={{0,0},{1,1},{2,16},{3,17},{4,32},{5,33},{6,48},{7,49},{8,64},{9,65... | collective-permute-start | bytes 1769480 | tf_op jit(solution)/shard_map/ppermute | solution.py:59
  225.2 29.1 %collective-permute-start.8 = (f32[384,384]{1,0:T(8,128)S(1)}, f32[384,384]{1,0:T(8,128)S(1)}, u32[]{:S(2)}, u32[]{:S(2)}) collective-permute-start(f32[384,384]{1,0:T(8,128)S(1)} %fusion.8), channel_id=1, source_target_pairs={{0,32},{32,64},{64,96},{96,0},{1,33},{33,65},{65,97},{97,1},{2,34}... | collective-permute-start | bytes 1769480 | tf_op jit(solution)/shard_map/ppermute | solution.py:15
  229.4 26.1 %collective-permute-start.9 = (f32[384,384]{1,0:T(8,128)S(1)}, f32[384,384]{1,0:T(8,128)S(1)}, u32[]{:S(2)}, u32[]{:S(2)}) collective-permute-start(f32[384,384]{1,0:T(8,128)S(1)} %fusion.8), channel_id=1, source_target_pairs={{0,96},{32,0},{64,32},{96,64},{1,97},{33,1},{65,33},{97,65},{2,98}... | collective-permute-start | bytes 1769480 | tf_op jit(solution)/shard_map/ppermute | solution.py:15
  233.8 32.0 %collective-permute-start.12 = (f32[384,384]{1,0:T(8,128)S(1)}, f32[384,384]{1,0:T(8,128)S(1)}, u32[]{:S(2)}, u32[]{:S(2)}) collective-permute-start(f32[384,384]{1,0:T(8,128)S(1)} %fusion.8), channel_id=1, source_target_pairs={{0,16},{16,0},{1,17},{17,1},{2,18},{18,2},{3,19},{19,3},{4,20},{20... | collective-permute-start | bytes 1769480 | tf_op jit(solution)/shard_map/ppermute | solution.py:15
  254.4 10.1 %collective-permute-start.10 = (f32[192,384]{1,0:T(8,128)S(1)}, f32[192,384]{1,0:T(8,128)S(1)}, u32[]{:S(2)}, u32[]{:S(2)}) collective-permute-start(f32[192,384]{1,0:T(8,128)S(1)} %slice.202), channel_id=1, source_target_pairs={{0,32},{32,64},{64,96},{96,0},{1,33},{33,65},{65,97},{97,1},{2,34}... | collective-permute-start | bytes 884744 | tf_op jit(solution)/shard_map/ppermute | solution.py:15
  255.5 8.9 %collective-permute-start.11 = (f32[192,384]{1,0:T(8,128)S(1)}, f32[192,384]{1,0:T(8,128)S(1)}, u32[]{:S(2)}, u32[]{:S(2)}) collective-permute-start(f32[192,384]{1,0:T(8,128)S(1)} %slice.203), channel_id=1, source_target_pairs={{0,96},{32,0},{64,32},{96,64},{1,97},{33,1},{65,33},{97,65},{2,98}... | collective-permute-start | bytes 884744 | tf_op jit(solution)/shard_map/ppermute | solution.py:15
  259.3 6.5 %collective-permute-start.13 = (f32[384,384]{1,0:T(8,128)S(1)}, f32[384,384]{1,0:T(8,128)S(1)}, u32[]{:S(2)}, u32[]{:S(2)}) collective-permute-start(f32[384,384]{1,0:T(8,128)S(1)} %collective-permute-done.8), channel_id=1, source_target_pairs={{0,16},{16,0},{1,17},{17,1},{2,18},{18,2},{3,19},{19,3},{4,20},{20... | collective-permute-start | bytes 1769480 | tf_op jit(solution)/shard_map/ppermute | solution.py:15
  259.9 6.0 %collective-permute-start.14 = (f32[384,384]{1,0:T(8,128)S(1)}, f32[384,384]{1,0:T(8,128)S(1)}, u32[]{:S(2)}, u32[]{:S(2)}) collective-permute-start(f32[384,384]{1,0:T(8,128)S(1)} %collective-permute-done.9), channel_id=1, source_target_pairs={{0,16},{16,0},{1,17},{17,1},{2,18},{18,2},{3,19},{19,3},{4,20},{20... | collective-permute-start | bytes 1769480 | tf_op jit(solution)/shard_map/ppermute | solution.py:15
  264.5 2.7 collective-permute-start.15
  274.9 16.9 %collective-permute-start.17 = (f32[384,384]{1,0:T(8,128)S(1)}, f32[384,384]{1,0:T(8,128)S(1)}, u32[]{:S(2)}, u32[]{:S(2)}) collective-permute-start(f32[384,384]{1,0:T(8,128)S(1)} %get-tuple-element.41), channel_id=1, source_target_pairs={{0,32},{32,64},{64,96},{96,0},{1,33},{33,65},{65,97},{97,1},{2,34}... | collective-permute-start | bytes 1769480 | tf_op jit(solution)/shard_map/ppermute | solution.py:15
  275.4 16.7 %collective-permute-start.18 = (f32[384,384]{1,0:T(8,128)S(1)}, f32[384,384]{1,0:T(8,128)S(1)}, u32[]{:S(2)}, u32[]{:S(2)}) collective-permute-start(f32[384,384]{1,0:T(8,128)S(1)} %get-tuple-element.41), channel_id=1, source_target_pairs={{0,96},{32,0},{64,32},{96,64},{1,97},{33,1},{65,33},{97,65},{2,98}... | collective-permute-start | bytes 1769480 | tf_op jit(solution)/shard_map/ppermute | solution.py:15
  278.2 34.5 %collective-permute-start.21 = (f32[384,384]{1,0:T(8,128)S(1)}, f32[384,384]{1,0:T(8,128)}, u32[]{:S(2)}, u32[]{:S(2)}) collective-permute-start(f32[384,384]{1,0:T(8,128)S(1)} %get-tuple-element.41), channel_id=1, source_target_pairs={{0,16},{16,0},{1,17},{17,1},{2,18},{18,2},{3,19},{19,3},{4,20},{20... | collective-permute-start | bytes 1769480 | tf_op jit(solution)/shard_map/ppermute | solution.py:15
  280.5 34.1 %all-to-all-start.2 = ((f32[8,3,32,384]{3,2,1,0:T(8,128)}), f32[8,3,32,384]{3,2,1,0:T(8,128)S(1)}, u32[]{:S(2)}, u32[]{:S(2)}) async-start(f32[8,3,32,384]{3,2,1,0:T(8,128)} %broadcast_select_fusion), calls=%async_computation.2 | async-start | bytes 2359296 | tf_op jit(solution)/shard_map/all_to_all | solution.py:82
  291.8 18.9 %collective-permute-start.19 = (f32[192,384]{1,0:T(8,128)S(1)}, f32[192,384]{1,0:T(8,128)S(1)}, u32[]{:S(2)}, u32[]{:S(2)}) collective-permute-start(f32[192,384]{1,0:T(8,128)S(1)} %slice.205), channel_id=1, source_target_pairs={{0,32},{32,64},{64,96},{96,0},{1,33},{33,65},{65,97},{97,1},{2,34}... | collective-permute-start | bytes 884744 | tf_op jit(solution)/shard_map/ppermute | solution.py:15
  292.0 18.7 %collective-permute-start.20 = (f32[192,384]{1,0:T(8,128)S(1)}, f32[192,384]{1,0:T(8,128)S(1)}, u32[]{:S(2)}, u32[]{:S(2)}) collective-permute-start(f32[192,384]{1,0:T(8,128)S(1)} %slice.206), channel_id=1, source_target_pairs={{0,96},{32,0},{64,32},{96,64},{1,97},{33,1},{65,33},{97,65},{2,98}... | collective-permute-start | bytes 884744 | tf_op jit(solution)/shard_map/ppermute | solution.py:15
  295.8 20.0 %collective-permute-start.22 = (f32[384,384]{1,0:T(8,128)S(1)}, f32[384,384]{1,0:T(8,128)}, u32[]{:S(2)}, u32[]{:S(2)}) collective-permute-start(f32[384,384]{1,0:T(8,128)S(1)} %collective-permute-done.17), channel_id=1, source_target_pairs={{0,16},{16,0},{1,17},{17,1},{2,18},{18,2},{3,19},{19,3},{4,20},{20... | collective-permute-start | bytes 1769480 | tf_op jit(solution)/shard_map/ppermute | solution.py:15
  297.9 19.7 %collective-permute-start.23 = (f32[384,384]{1,0:T(8,128)S(1)}, f32[384,384]{1,0:T(8,128)}, u32[]{:S(2)}, u32[]{:S(2)}) collective-permute-start(f32[384,384]{1,0:T(8,128)S(1)} %collective-permute-done.18), channel_id=1, source_target_pairs={{0,16},{16,0},{1,17},{17,1},{2,18},{18,2},{3,19},{19,3},{4,20},{20... | collective-permute-start | bytes 1769480 | tf_op jit(solution)/shard_map/ppermute | solution.py:15
  310.8 8.8 %collective-permute-start.24 = (f32[384,384]{1,0:T(8,128)S(1)}, f32[384,384]{1,0:T(8,128)}, u32[]{:S(2)}, u32[]{:S(2)}) collective-permute-start(f32[384,384]{1,0:T(8,128)S(1)} %constant_dynamic-update-slice_fusion.52), channel_id=1, source_target_pairs={{0,16},{16,0},{1,17},{17,1},{2,18},{18,2},{3,19},{19,3},{4,20},{20... | collective-permute-start | bytes 1769480 | tf_op jit(solution)/shard_map/ppermute | solution.py:15
  (6 other events, 24.8 us)
Sparse Core Ops, SparseCore 0:
  60.3 77.9 all-gather.6
  141.0 100.0 all-gather.4
  243.3 75.4 all-gather.8
where the time goes:
time: 345 us; the launch traced here: 343 us
  waiting for transfers between devices  102 us (30%)
  between operations  89 us (26%)
  starting transfers between devices  62.1 us (18%)
  local copies, waits for them, and re-layouts  56.3 us (16%)
  matrix products  30.6 us (9%)
    ppermute x24, waiting for transfers between devices, shift(): return lax.ppermute(x, axis, [(i, (i + k) % n) for i in range(n)])  61.1 us
    ppermute x24, starting transfers between devices, shift(): return lax.ppermute(x, axis, [(i, (i + k) % n) for i in range(n)])  43.1 us
    dot_general x4, matrix products, dot(): lax.dot_general(a, b, (dims, ((), ())), precision=lax.Precision.HIGH, pre...  30.6 us
    dynamic_update_slice x8, local copies, waits for them, and re-layouts, per_device(): strip = lax.dynamic_update_slice(strip, t, (r * h, 0))  15.4 us
    all_to_all x2, waiting for transfers between devices, spread(): lax.all_to_all(x.reshape(3, 8, sub, w), ROW, 1, 0, tiled=True)  15.4 us
    unnamed x72, local copies, waits for them, and re-layouts  14.6 us
    ppermute x1, waiting for transfers between devices, per_device(): lax.ppermute(u, ALL, [(16 * r + c, 16 * (c // 2) + 2 * r + c % 2) for r i...  14.5 us
    all_gather x1, waiting for transfers between devices, per_device(): f_all = lax.all_gather(f, COL, axis=1, tiled=True)  11.1 us
  transfers between devices with their start and end apart: 31, of which 10 were waited for; matrix products, arithmetic and copies ran while one was open for 20% of the time, Pallas kernels for 0%

commit v1 on v0

--- a/solution.py
+++ b/solution.py
@@ -49,12 +49,15 @@
     sub = h // 24
     part = NANC * sub
     f = pick(spread(factor_cross), ancestors).reshape(part, w)
-    f_all = lax.all_gather(f, COL, axis=1, tiled=True)
     strip = jnp.zeros((8 * h, w), jnp.float32)
     for r, t in gather_rows(factor_inverse):
         strip = lax.dynamic_update_slice(strip, t, (r * h, 0))
     s = pick(spread(sigma_top), ancestors).reshape(part, w)
-    s_all = lax.all_gather(s, COL, axis=1, tiled=True)
+    f_all, s_all = jnp.split(
+        lax.all_gather(jnp.concatenate([f, s], axis=0), COL, axis=1, tiled=True),
+        [f.shape[0]],
+        axis=0,
+    )
     u = dot(f_all, strip, ((1,), (0,)))
     moved = lax.ppermute(
         u, ALL, [(16 * r + c, 16 * (c // 2) + 2 * r + c % 2) for r in range(8) for c in range(16)]

time: 345 us -> 385 us (1.12)
  waiting for transfers between devices: 102 us -> 139 us
  starting transfers between devices: 62.1 us -> 73.6 us
  local copies, waits for them, and re-layouts: 56.3 us -> 46.9 us
    all_gather x2 -> x1, waiting for transfers between devices: 11.1 us -> 58.5 us  [per_device(): lax.all_gather(jnp.concatenate([f, s], axis=0), COL, axis=1, tiled=True)]
    unnamed x72 -> x68, local copies, waits for them, and re-layouts: 14.6 us -> 1.92 us
    ppermute x24, starting transfers between devices: 43.1 us -> 54.6 us  [shift(): return lax.ppermute(x, axis, [(i, (i + k) % n) for i in range(n)])]
    ppermute x1, waiting for transfers between devices: 14.5 us -> 7.57 us  [per_device(): lax.ppermute(u, ALL, [(16 * r + c, 16 * (c // 2) + 2 * r + c % 2) for r i...]
    split x0 -> x1, local copies, waits for them, and re-layouts: none -> 4.45 us  [per_device(): jnp.split(lax.all_gather(jnp.concatenate([f, s], axis=0), COL, axis=1, ti...]
  transfers between devices with their start and end apart: 31 -> 30, of which waited for: 10 -> 9; matrix products, arithmetic and copies ran while one was open for 20% -> 13% of each run, Pallas kernels for 0% -> 0%
where the time goes in v1:
time: 385 us; the launch traced here: 383 us
  waiting for transfers between devices  139 us (36%)
  between operations  88.9 us (23%)
  starting transfers between devices  73.6 us (19%)
  local copies, waits for them, and re-layouts  46.9 us (12%)
  matrix products  30.6 us (8%)
  other arithmetic  4.08 us (1%)
    all_gather x1, waiting for transfers between devices, per_device(): lax.all_gather(jnp.concatenate([f, s], axis=0), COL, axis=1, tiled=True)  58.5 us
    ppermute x24, waiting for transfers between devices, shift(): return lax.ppermute(x, axis, [(i, (i + k) % n) for i in range(n)])  57.6 us
    ppermute x24, starting transfers between devices, shift(): return lax.ppermute(x, axis, [(i, (i + k) % n) for i in range(n)])  54.6 us
    dot_general x4, matrix products, dot(): lax.dot_general(a, b, (dims, ((), ())), precision=lax.Precision.HIGH, pre...  30.6 us
    all_to_all x2, waiting for transfers between devices, spread(): lax.all_to_all(x.reshape(3, 8, sub, w), ROW, 1, 0, tiled=True)  15.4 us
    dynamic_update_slice x8, local copies, waits for them, and re-layouts, per_device(): strip = lax.dynamic_update_slice(strip, t, (r * h, 0))  15.4 us
    all_to_all x2, starting transfers between devices, spread(): lax.all_to_all(x.reshape(3, 8, sub, w), ROW, 1, 0, tiled=True)  10.3 us
    dynamic_update_slice x7, local copies, waits for them, and re-layouts, per_device(): sigma_col = lax.dynamic_update_slice(sigma_col, t[None], (r, 0, 0))  10.3 us
  transfers between devices with their start and end apart: 30, of which 9 were waited for; matrix products, arithmetic and copies ran while one was open for 13% of the time, Pallas kernels for 0%

profile of v1, /device:TPU:1, one launch (start us, length us, event | category | flops | bytes accessed | tf_op | source)
XLA Modules:
  0.0 383.1 jit_solution(962950729751355335)
XLA Ops:
  7.2 2.5 copy.63
  9.6 6.0 %all-to-all-start.1 = ((f32[3,8,32,384]{3,2,0,1:T(8,128)}), f32[3,8,32,384]{3,2,0,1:T(8,128)S(1)}, u32[]{:S(2)}, u32[]{:S(2)}) async-start(f32[3,8,32,384]{3,2,0,1:T(8,128)} %copy.63), calls=%async_computation.1 | async-start | bytes 2359296 | tf_op jit(solution)/shard_map/all_to_all | solution.py:34
  16.7 15.4 %all-to-all-done.1 = f32[3,8,32,384]{3,2,0,1:T(8,128)S(1)} async-done(((f32[3,8,32,384]{3,2,0,1:T(8,128)}), f32[3,8,32,384]{3,2,0,1:T(8,128)S(1)}, u32[]{:S(2)}, u32[]{:S(2)}) %all-to-all-start.1) | async-done | bytes 1179680 | tf_op jit(solution)/shard_map/all_to_all | solution.py:34
  32.1 4.3 %all-to-all-start = ((f32[3,8,32,384]{3,2,0,1:T(8,128)}), f32[3,8,32,384]{3,2,0,1:T(8,128)S(1)}, u32[]{:S(2)}, u32[]{:S(2)}) async-start(f32[3,8,32,384]{3,2,0,1:T(8,128)} %copy.62), calls=%async_computation | async-start | bytes 2359296 | tf_op jit(solution)/shard_map/all_to_all | solution.py:34
  63.3 26.2 %collective-permute-done = f32[768,384]{1,0:T(8,128)S(1)} collective-permute-done((f32[768,384]{1,0:T(8,128)}, f32[768,384]{1,0:T(8,128)S(1)}, u32[]{:S(2)}, u32[]{:S(2)}) %collective-permute-start) | collective-permute-done | bytes 1179680 | tf_op jit(solution)/shard_map/ppermute | solution.py:15
  89.7 2.7 collective-permute-start.3
  94.3 10.5 %collective-permute-done.2 = f32[384,384]{1,0:T(8,128)S(1)} collective-permute-done((f32[384,384]{1,0:T(8,128)S(1)}, f32[384,384]{1,0:T(8,128)S(1)}, u32[]{:S(2)}, u32[]{:S(2)}) %collective-permute-start.2) | collective-permute-done | bytes 589856 | tf_op jit(solution)/shard_map/ppermute | solution.py:15
  106.8 4.3 %broadcast_in_dim.53 = f32[6144,384]{1,0:T(8,128)} broadcast(f32[]{:T(128)} %constant.74.clone.1), dimensions={} | broadcast | bytes 9437188 | tf_op jit(solution)/shard_map/broadcast_in_dim | solution.py:52
  116.8 2.4 constant_dynamic-update-slice_fusion.65
  119.2 2.4 constant_dynamic-update-slice_fusion.64
  124.0 2.4 constant_dynamic-update-slice_fusion.62
  126.4 58.5 %all-gather.4.cloned.1.call-done = f32[768,6144]{1,0:T(8,128)} async-done(((f32[768,384]{1,0:T(8,128)}), f32[768,6144]{1,0:T(8,128)}) %all-gather.4.cloned.1.call-update) | async-done | bytes 18874384 | tf_op jit(solution)/shard_map/all_gather | solution.py:57
  184.9 11.7 %fusion = f32[384,384]{1,0:T(8,128)S(1)} fusion(f32[6144,384]{1,0:T(8,128)} %constant_dynamic-update-slice_fusion.62, f32[768,6144]{1,0:T(8,128)} %all-gather.4.cloned.1.call-done), kind=kOutput, calls=%fused_computation | convolution fusion | flops 5435817984 | bytes 19464192 | tf_op jit(solution)/shard_map/dot_general | solution.py:42
  196.6 5.1 %collective-permute-start.16 = (f32[384,384]{1,0:T(8,128)S(1)}, f32[384,384]{1,0:T(8,128)S(1)}, u32[]{:S(2)}, u32[]{:S(2)}) collective-permute-start(f32[384,384]{1,0:T(8,128)S(1)} %fusion), channel_id=1, source_target_pairs={{0,0},{1,1},{2,16},{3,17},{4,32},{5,33},{6,48},{7,49},{8,64},{9,65... | collective-permute-start | bytes 1769480 | tf_op jit(solution)/shard_map/ppermute | solution.py:62
  201.7 7.6 %collective-permute-done.16 = f32[384,384]{1,0:T(8,128)S(1)} collective-permute-done((f32[384,384]{1,0:T(8,128)S(1)}, f32[384,384]{1,0:T(8,128)S(1)}, u32[]{:S(2)}, u32[]{:S(2)}) %collective-permute-start.16) | collective-permute-done | bytes 589856 | tf_op jit(solution)/shard_map/ppermute | solution.py:62
  264.6 7.6 %collective-permute-start.8 = (f32[384,384]{1,0:T(8,128)S(1)}, f32[384,384]{1,0:T(8,128)S(1)}, u32[]{:S(2)}, u32[]{:S(2)}) collective-permute-start(f32[384,384]{1,0:T(8,128)S(1)} %fusion), channel_id=1, source_target_pairs={{0,32},{32,64},{64,96},{96,0},{1,33},{33,65},{65,97},{97,1},{2,34}... | collective-permute-start | bytes 1769480 | tf_op jit(solution)/shard_map/ppermute | solution.py:15
  272.2 5.2 %collective-permute-start.9 = (f32[384,384]{1,0:T(8,128)S(1)}, f32[384,384]{1,0:T(8,128)S(1)}, u32[]{:S(2)}, u32[]{:S(2)}) collective-permute-start(f32[384,384]{1,0:T(8,128)S(1)} %fusion), channel_id=1, source_target_pairs={{0,96},{32,0},{64,32},{96,64},{1,97},{33,1},{65,33},{97,65},{2,98}... | collective-permute-start | bytes 1769480 | tf_op jit(solution)/shard_map/ppermute | solution.py:15
  277.4 12.1 %collective-permute-start.12 = (f32[384,384]{1,0:T(8,128)S(1)}, f32[384,384]{1,0:T(8,128)S(1)}, u32[]{:S(2)}, u32[]{:S(2)}) collective-permute-start(f32[384,384]{1,0:T(8,128)S(1)} %fusion), channel_id=1, source_target_pairs={{0,16},{16,0},{1,17},{17,1},{2,18},{18,2},{3,19},{19,3},{4,20},{20... | collective-permute-start | bytes 1769480 | tf_op jit(solution)/shard_map/ppermute | solution.py:15
  289.5 4.5 %split.8 = f32[384,6144]{1,0:T(8,128)S(1)} slice(f32[768,6144]{1,0:T(8,128)} %all-gather.4.cloned.1.call-done), slice={[384:768], [0:6144]} | slice | bytes 18874368 | tf_op jit(solution)/shard_map/split | solution.py:56
  295.3 2.7 collective-permute-start.11
  298.1 2.8 collective-permute-start.13
  302.9 3.1 collective-permute-start.15
  307.7 2.5 broadcast_in_dim.55
  310.2 5.0 %bitcast_dynamic-update-slice_fusion.7 = (f32[8,384,384]{2,1,0:T(8,128)}, f32[384,384]{1,0:T(8,128)S(1)}) fusion(f32[8,384,384]{2,1,0:T(8,128)} %broadcast_in_dim.55, s32[]{:T(128)S(6)} %select_n.283, f32[384,3072]{1,0:T(8,128)S(1)} %dynamic-slice_dynamic-update-slice_fusion, f32[3072,384]{1,0:T(8,128)S(1)} %bitcast.118), kind=kOutput, calls=%fused_computation.18 | convolution fusion | flops 2718056448 | bytes 10616836 | tf_op jit(solution)/shard_map/dot_general | solution.py:42
  315.4 2.6 collective-permute-start.18
  320.5 3.5 all-to-all-start.2
  324.0 7.2 %collective-permute-done.17 = f32[384,384]{1,0:T(8,128)S(1)} collective-permute-done((f32[384,384]{1,0:T(8,128)S(1)}, f32[384,384]{1,0:T(8,128)S(1)}, u32[]{:S(2)}, u32[]{:S(2)}) %collective-permute-start.17) | collective-permute-done | bytes 589856 | tf_op jit(solution)/shard_map/ppermute | solution.py:15
  331.4 3.8 collective-permute-start.20
  335.2 2.7 collective-permute-start.22
  339.6 10.5 %collective-permute-done.19 = f32[192,384]{1,0:T(8,128)S(1)} collective-permute-done((f32[192,384]{1,0:T(8,128)S(1)}, f32[192,384]{1,0:T(8,128)S(1)}, u32[]{:S(2)}, u32[]{:S(2)}) %collective-permute-start.19) | collective-permute-done | bytes 294944 | tf_op jit(solution)/shard_map/ppermute | solution.py:15
  361.3 7.8 %fusion.4 = f32[384,384]{1,0:T(8,128)S(1)} fusion(f32[8,384,384]{2,1,0:T(8,128)} %bitcast_dynamic-update-slice_fusion, f32[8,2,384,384]{3,2,1,0:T(8,128)} %bitcast.119), kind=kOutput, calls=%fused_computation.6 | convolution fusion | flops 2717908992 | bytes 10027008 | tf_op jit(solution)/shard_map/dot_general | solution.py:42
  369.0 6.1 %fusion.5 = f32[384,384]{1,0:T(8,128)S(1)} fusion(f32[8,384,384]{2,1,0:T(8,128)} %bitcast_dynamic-update-slice_fusion, f32[8,2,384,384]{3,2,1,0:T(8,128)S(1)} %bitcast.120), kind=kOutput, calls=%fused_computation.7 | convolution fusion | flops 2717908992 | bytes 10027008 | tf_op jit(solution)/shard_map/dot_general | solution.py:42
  (154 shorter events, 42.5 us)
Async XLA Ops:
  7.2 8.4 %copy-start.2 = (f32[768,384]{1,0:T(8,128)S(1)}, f32[768,384]{1,0:T(8,128)}, u32[]{:S(2)}) copy-start(f32[768,384]{1,0:T(8,128)} %param.6) | copy-start | bytes 3538948
  7.2 29.3 %copy-start.4 = (s32[12]{0:T(128)S(1)}, s32[12]{0:T(128)}, u32[]{:S(2)}) copy-start(s32[12]{0:T(128)} %param.9) | copy-start | bytes 148
  9.6 22.5 %all-to-all-start.1 = ((f32[3,8,32,384]{3,2,0,1:T(8,128)}), f32[3,8,32,384]{3,2,0,1:T(8,128)S(1)}, u32[]{:S(2)}, u32[]{:S(2)}) async-start(f32[3,8,32,384]{3,2,0,1:T(8,128)} %copy.63), calls=%async_computation.1 | async-start | bytes 2359296 | tf_op jit(solution)/shard_map/all_to_all | solution.py:34
  32.1 26.7 %all-to-all-start = ((f32[3,8,32,384]{3,2,0,1:T(8,128)}), f32[3,8,32,384]{3,2,0,1:T(8,128)S(1)}, u32[]{:S(2)}, u32[]{:S(2)}) async-start(f32[3,8,32,384]{3,2,0,1:T(8,128)} %copy.62), calls=%async_computation | async-start | bytes 2359296 | tf_op jit(solution)/shard_map/all_to_all | solution.py:34
  36.5 148.4 %all-gather.4.cloned.1.call-start = ((), (), s32[]{:S(2)}) async-start(), calls=%async_computation.3 | async-start | bytes 20054016 | tf_op jit(solution)/shard_map/all_gather | solution.py:57
  60.4 300.8 %all-gather.6.cloned.1.call-start = ((), (), s32[]{:S(2)}) async-start(), calls=%async_computation.4 | async-start | bytes 10027008 | tf_op jit(solution)/shard_map/all_gather | solution.py:65
  60.5 29.0 %collective-permute-start = (f32[768,384]{1,0:T(8,128)}, f32[768,384]{1,0:T(8,128)S(1)}, u32[]{:S(2)}, u32[]{:S(2)}) collective-permute-start(f32[768,384]{1,0:T(8,128)} %param.7), channel_id=1, source_target_pairs={{0,32},{32,64},{64,96},{96,0},{1,33},{33,65},{65,97},{97,1},{2,34}... | collective-permute-start | bytes 3538952 | tf_op jit(solution)/shard_map/ppermute | solution.py:15
  62.0 27.7 %collective-permute-start.1 = (f32[768,384]{1,0:T(8,128)}, f32[768,384]{1,0:T(8,128)S(1)}, u32[]{:S(2)}, u32[]{:S(2)}) collective-permute-start(f32[768,384]{1,0:T(8,128)} %param.7), channel_id=1, source_target_pairs={{0,96},{32,0},{64,32},{96,64},{1,97},{33,1},{65,33},{97,65},{2,98}... | collective-permute-start | bytes 3538952 | tf_op jit(solution)/shard_map/ppermute | solution.py:15
  89.6 15.3 %collective-permute-start.2 = (f32[384,384]{1,0:T(8,128)S(1)}, f32[384,384]{1,0:T(8,128)S(1)}, u32[]{:S(2)}, u32[]{:S(2)}) collective-permute-start(f32[384,384]{1,0:T(8,128)S(1)} %slice.200), channel_id=1, source_target_pairs={{0,32},{32,64},{64,96},{96,0},{1,33},{33,65},{65,97},{97,1},{2,34}... | collective-permute-start | bytes 1769480 | tf_op jit(solution)/shard_map/ppermute | solution.py:15
  89.7 15.2 %collective-permute-start.3 = (f32[384,384]{1,0:T(8,128)S(1)}, f32[384,384]{1,0:T(8,128)S(1)}, u32[]{:S(2)}, u32[]{:S(2)}) collective-permute-start(f32[384,384]{1,0:T(8,128)S(1)} %slice.201), channel_id=1, source_target_pairs={{0,96},{32,0},{64,32},{96,64},{1,97},{33,1},{65,33},{97,65},{2,98}... | collective-permute-start | bytes 1769480 | tf_op jit(solution)/shard_map/ppermute | solution.py:15
  92.4 24.4 %collective-permute-start.4 = (f32[768,384]{1,0:T(8,128)}, f32[768,384]{1,0:T(8,128)}, u32[]{:S(2)}, u32[]{:S(2)}) collective-permute-start(f32[768,384]{1,0:T(8,128)} %param.7), channel_id=1, source_target_pairs={{0,16},{16,0},{1,17},{17,1},{2,18},{18,2},{3,19},{19,3},{4,20},{20... | collective-permute-start | bytes 3538952 | tf_op jit(solution)/shard_map/ppermute | solution.py:15
  93.8 25.4 %collective-permute-start.5 = (f32[768,384]{1,0:T(8,128)S(1)}, f32[768,384]{1,0:T(8,128)}, u32[]{:S(2)}, u32[]{:S(2)}) collective-permute-start(f32[768,384]{1,0:T(8,128)S(1)} %collective-permute-done), channel_id=1, source_target_pairs={{0,16},{16,0},{1,17},{17,1},{2,18},{18,2},{3,19},{19,3},{4,20},{20... | collective-permute-start | bytes 3538952 | tf_op jit(solution)/shard_map/ppermute | solution.py:15
  93.8 27.8 %collective-permute-start.6 = (f32[768,384]{1,0:T(8,128)S(1)}, f32[768,384]{1,0:T(8,128)}, u32[]{:S(2)}, u32[]{:S(2)}) collective-permute-start(f32[768,384]{1,0:T(8,128)S(1)} %collective-permute-done.1), channel_id=1, source_target_pairs={{0,16},{16,0},{1,17},{17,1},{2,18},{18,2},{3,19},{19,3},{4,20},{20... | collective-permute-start | bytes 3538952 | tf_op jit(solution)/shard_map/ppermute | solution.py:15
  104.9 19.1 %collective-permute-start.7 = (f32[768,384]{1,0:T(8,128)S(1)}, f32[768,384]{1,0:T(8,128)}, u32[]{:S(2)}, u32[]{:S(2)}) collective-permute-start(f32[768,384]{1,0:T(8,128)S(1)} %constant_dynamic-update-slice_fusion.24), channel_id=1, source_target_pairs={{0,16},{16,0},{1,17},{17,1},{2,18},{18,2},{3,19},{19,3},{4,20},{20... | collective-permute-start | bytes 3538952 | tf_op jit(solution)/shard_map/ppermute | solution.py:15
  196.6 12.7 %collective-permute-start.16 = (f32[384,384]{1,0:T(8,128)S(1)}, f32[384,384]{1,0:T(8,128)S(1)}, u32[]{:S(2)}, u32[]{:S(2)}) collective-permute-start(f32[384,384]{1,0:T(8,128)S(1)} %fusion), channel_id=1, source_target_pairs={{0,0},{1,1},{2,16},{3,17},{4,32},{5,33},{6,48},{7,49},{8,64},{9,65... | collective-permute-start | bytes 1769480 | tf_op jit(solution)/shard_map/ppermute | solution.py:62
  264.6 30.5 %collective-permute-start.8 = (f32[384,384]{1,0:T(8,128)S(1)}, f32[384,384]{1,0:T(8,128)S(1)}, u32[]{:S(2)}, u32[]{:S(2)}) collective-permute-start(f32[384,384]{1,0:T(8,128)S(1)} %fusion), channel_id=1, source_target_pairs={{0,32},{32,64},{64,96},{96,0},{1,33},{33,65},{65,97},{97,1},{2,34}... | collective-permute-start | bytes 1769480 | tf_op jit(solution)/shard_map/ppermute | solution.py:15
  272.2 23.1 %collective-permute-start.9 = (f32[384,384]{1,0:T(8,128)S(1)}, f32[384,384]{1,0:T(8,128)S(1)}, u32[]{:S(2)}, u32[]{:S(2)}) collective-permute-start(f32[384,384]{1,0:T(8,128)S(1)} %fusion), channel_id=1, source_target_pairs={{0,96},{32,0},{64,32},{96,64},{1,97},{33,1},{65,33},{97,65},{2,98}... | collective-permute-start | bytes 1769480 | tf_op jit(solution)/shard_map/ppermute | solution.py:15
  277.4 28.7 %collective-permute-start.12 = (f32[384,384]{1,0:T(8,128)S(1)}, f32[384,384]{1,0:T(8,128)S(1)}, u32[]{:S(2)}, u32[]{:S(2)}) collective-permute-start(f32[384,384]{1,0:T(8,128)S(1)} %fusion), channel_id=1, source_target_pairs={{0,16},{16,0},{1,17},{17,1},{2,18},{18,2},{3,19},{19,3},{4,20},{20... | collective-permute-start | bytes 1769480 | tf_op jit(solution)/shard_map/ppermute | solution.py:15
  295.2 7.7 %collective-permute-start.10 = (f32[192,384]{1,0:T(8,128)S(1)}, f32[192,384]{1,0:T(8,128)S(1)}, u32[]{:S(2)}, u32[]{:S(2)}) collective-permute-start(f32[192,384]{1,0:T(8,128)S(1)} %slice.202), channel_id=1, source_target_pairs={{0,32},{32,64},{64,96},{96,0},{1,33},{33,65},{65,97},{97,1},{2,34}... | collective-permute-start | bytes 884744 | tf_op jit(solution)/shard_map/ppermute | solution.py:15
  295.3 7.6 %collective-permute-start.11 = (f32[192,384]{1,0:T(8,128)S(1)}, f32[192,384]{1,0:T(8,128)S(1)}, u32[]{:S(2)}, u32[]{:S(2)}) collective-permute-start(f32[192,384]{1,0:T(8,128)S(1)} %slice.203), channel_id=1, source_target_pairs={{0,96},{32,0},{64,32},{96,64},{1,97},{33,1},{65,33},{97,65},{2,98}... | collective-permute-start | bytes 884744 | tf_op jit(solution)/shard_map/ppermute | solution.py:15
  298.1 8.1 %collective-permute-start.13 = (f32[384,384]{1,0:T(8,128)S(1)}, f32[384,384]{1,0:T(8,128)S(1)}, u32[]{:S(2)}, u32[]{:S(2)}) collective-permute-start(f32[384,384]{1,0:T(8,128)S(1)} %collective-permute-done.8), channel_id=1, source_target_pairs={{0,16},{16,0},{1,17},{17,1},{2,18},{18,2},{3,19},{19,3},{4,20},{20... | collective-permute-start | bytes 1769480 | tf_op jit(solution)/shard_map/ppermute | solution.py:15
  300.9 5.4 %collective-permute-start.14 = (f32[384,384]{1,0:T(8,128)S(1)}, f32[384,384]{1,0:T(8,128)S(1)}, u32[]{:S(2)}, u32[]{:S(2)}) collective-permute-start(f32[384,384]{1,0:T(8,128)S(1)} %collective-permute-done.9), channel_id=1, source_target_pairs={{0,16},{16,0},{1,17},{17,1},{2,18},{18,2},{3,19},{19,3},{4,20},{20... | collective-permute-start | bytes 1769480 | tf_op jit(solution)/shard_map/ppermute | solution.py:15
  302.9 4.7 %collective-permute-start.15 = (f32[384,384]{1,0:T(8,128)S(1)}, f32[384,384]{1,0:T(8,128)S(1)}, u32[]{:S(2)}, u32[]{:S(2)}) collective-permute-start(f32[384,384]{1,0:T(8,128)S(1)} %constant_dynamic-update-slice_fusion.26), channel_id=1, source_target_pairs={{0,16},{16,0},{1,17},{17,1},{2,18},{18,2},{3,19},{19,3},{4,20},{20... | collective-permute-start | bytes 1769480 | tf_op jit(solution)/shard_map/ppermute | solution.py:15
  315.2 16.0 %collective-permute-start.17 = (f32[384,384]{1,0:T(8,128)S(1)}, f32[384,384]{1,0:T(8,128)S(1)}, u32[]{:S(2)}, u32[]{:S(2)}) collective-permute-start(f32[384,384]{1,0:T(8,128)S(1)} %get-tuple-element.41), channel_id=1, source_target_pairs={{0,32},{32,64},{64,96},{96,0},{1,33},{33,65},{65,97},{97,1},{2,34}... | collective-permute-start | bytes 1769480 | tf_op jit(solution)/shard_map/ppermute | solution.py:15
  315.4 15.9 %collective-permute-start.18 = (f32[384,384]{1,0:T(8,128)S(1)}, f32[384,384]{1,0:T(8,128)S(1)}, u32[]{:S(2)}, u32[]{:S(2)}) collective-permute-start(f32[384,384]{1,0:T(8,128)S(1)} %get-tuple-element.41), channel_id=1, source_target_pairs={{0,96},{32,0},{64,32},{96,64},{1,97},{33,1},{65,33},{97,65},{2,98}... | collective-permute-start | bytes 1769480 | tf_op jit(solution)/shard_map/ppermute | solution.py:15
  318.0 34.5 %collective-permute-start.21 = (f32[384,384]{1,0:T(8,128)S(1)}, f32[384,384]{1,0:T(8,128)}, u32[]{:S(2)}, u32[]{:S(2)}) collective-permute-start(f32[384,384]{1,0:T(8,128)S(1)} %get-tuple-element.41), channel_id=1, source_target_pairs={{0,16},{16,0},{1,17},{17,1},{2,18},{18,2},{3,19},{19,3},{4,20},{20... | collective-permute-start | bytes 1769480 | tf_op jit(solution)/shard_map/ppermute | solution.py:15
  320.5 33.9 %all-to-all-start.2 = ((f32[8,3,32,384]{3,2,1,0:T(8,128)}), f32[8,3,32,384]{3,2,1,0:T(8,128)S(1)}, u32[]{:S(2)}, u32[]{:S(2)}) async-start(f32[8,3,32,384]{3,2,1,0:T(8,128)} %broadcast_select_fusion), calls=%async_computation.2 | async-start | bytes 2359296 | tf_op jit(solution)/shard_map/all_to_all | solution.py:85
  331.2 18.9 %collective-permute-start.19 = (f32[192,384]{1,0:T(8,128)S(1)}, f32[192,384]{1,0:T(8,128)S(1)}, u32[]{:S(2)}, u32[]{:S(2)}) collective-permute-start(f32[192,384]{1,0:T(8,128)S(1)} %slice.205), channel_id=1, source_target_pairs={{0,32},{32,64},{64,96},{96,0},{1,33},{33,65},{65,97},{97,1},{2,34}... | collective-permute-start | bytes 884744 | tf_op jit(solution)/shard_map/ppermute | solution.py:15
  331.4 18.8 %collective-permute-start.20 = (f32[192,384]{1,0:T(8,128)S(1)}, f32[192,384]{1,0:T(8,128)S(1)}, u32[]{:S(2)}, u32[]{:S(2)}) collective-permute-start(f32[192,384]{1,0:T(8,128)S(1)} %slice.206), channel_id=1, source_target_pairs={{0,96},{32,0},{64,32},{96,64},{1,97},{33,1},{65,33},{97,65},{2,98}... | collective-permute-start | bytes 884744 | tf_op jit(solution)/shard_map/ppermute | solution.py:15
  335.2 20.3 %collective-permute-start.22 = (f32[384,384]{1,0:T(8,128)S(1)}, f32[384,384]{1,0:T(8,128)}, u32[]{:S(2)}, u32[]{:S(2)}) collective-permute-start(f32[384,384]{1,0:T(8,128)S(1)} %collective-permute-done.17), channel_id=1, source_target_pairs={{0,16},{16,0},{1,17},{17,1},{2,18},{18,2},{3,19},{19,3},{4,20},{20... | collective-permute-start | bytes 1769480 | tf_op jit(solution)/shard_map/ppermute | solution.py:15
  337.9 19.5 %collective-permute-start.23 = (f32[384,384]{1,0:T(8,128)S(1)}, f32[384,384]{1,0:T(8,128)}, u32[]{:S(2)}, u32[]{:S(2)}) collective-permute-start(f32[384,384]{1,0:T(8,128)S(1)} %collective-permute-done.18), channel_id=1, source_target_pairs={{0,16},{16,0},{1,17},{17,1},{2,18},{18,2},{3,19},{19,3},{4,20},{20... | collective-permute-start | bytes 1769480 | tf_op jit(solution)/shard_map/ppermute | solution.py:15
  350.2 9.1 %collective-permute-start.24 = (f32[384,384]{1,0:T(8,128)S(1)}, f32[384,384]{1,0:T(8,128)}, u32[]{:S(2)}, u32[]{:S(2)}) collective-permute-start(f32[384,384]{1,0:T(8,128)S(1)} %constant_dynamic-update-slice_fusion.52), channel_id=1, source_target_pairs={{0,16},{16,0},{1,17},{17,1},{2,18},{18,2},{3,19},{19,3},{4,20},{20... | collective-permute-start | bytes 1769480 | tf_op jit(solution)/shard_map/ppermute | solution.py:15
  (3 other events, 14.7 us)
Sparse Core Ops, SparseCore 0:
  60.6 124.2 all-gather.3
  210.2 93.8 all-gather.5
